TPU v7x, 32 devices: a whole 2x2x4 slice. The times are simulated.
32 devices in a mesh: freq: 4 (over x, core), pos: 8 (over z, y).
Axes of the slice: x: 2, y: 2, z: 4, core: 2. Of those that a mesh axis runs over, the one named last changes fastest.
Arguments:
- spectra: bfloat16 [16, 2, 256, 8192], P(None, None, 'freq', 'pos'), may hold values from -6 to 6
- green: bfloat16 [16, 8192, 2048], P('freq', 'pos'), may hold values from -0.046875 to 0.046875
- recorded: bfloat16 [256, 1024, 512], P('pos', 'freq'), may hold values from -6 to 6
- filter_taps: float32 [256, 11], P('pos'), may hold values from -3 to 3
Outputs:
- primaries: bfloat16 [256, 1024, 512], P('pos', 'freq')
All inputs are finite; a program needn't handle non-finite values.
Results may differ from a plain program's by a relative error of at most 0.001.
Values may be sent and summed in bfloat16 or wider, within the bound.
A program may use at most 128 MiB of HBM per device.

v0:
```python
import jax
import jax.numpy as jnp
from jax import lax
from jax.sharding import PartitionSpec as P

BAND_START = 32


def phase_table(first_freq, freq_count, total_freqs, samples):
    bins = BAND_START + first_freq + jnp.arange(freq_count, dtype=jnp.int32)
    sample_index = jnp.arange(samples, dtype=jnp.int32)
    phase = bins[:, None] * sample_index[None, :] % samples
    angle = 2.0 * jnp.pi / samples * phase.astype(jnp.float32)
    scale = 1.0 / jnp.sqrt(jnp.float32(total_freqs))
    return jnp.stack([jnp.cos(angle), -jnp.sin(angle)], 1) * scale


def on_device(spectra, green, recorded, filter_taps):
    regrouped = lax.all_to_all(spectra, "freq", split_axis=0, concat_axis=2, tiled=True)
    half_cols = green.shape[2] // 2
    shot_count = regrouped.shape[2]
    own_rows = shot_count // lax.axis_size("pos")
    product = jnp.einsum("fisk,fkr->sfir", regrouped, green, preferred_element_type=jnp.float32)
    real_part = product[:, :, 0, :half_cols] - product[:, :, 1, half_cols:]
    imag_part = product[:, :, 0, half_cols:] + product[:, :, 1, :half_cols]
    summed = lax.psum(jnp.stack([real_part, imag_part], 2), "pos")
    own_share = lax.dynamic_slice_in_dim(summed, lax.axis_index("pos") * own_rows, own_rows, 0)
    samples = recorded.shape[2]
    total_freqs = spectra.shape[0]
    spread = lax.all_to_all(own_share, "freq", split_axis=3, concat_axis=1, tiled=True)
    table = phase_table(0, total_freqs, total_freqs, samples)
    traces = jnp.einsum("sfir,fit->srt", spread, table, precision=lax.Precision.HIGHEST)
    tap_count = filter_taps.shape[1]
    margin = (tap_count - 1) // 2
    padded = jnp.pad(traces, ((0, 0), (0, 0), (margin, margin)))
    result = recorded.astype(jnp.float32)
    for lag in range(tap_count):
        result = result - filter_taps[:, lag][:, None, None] * padded[:, :, lag : lag + samples]
    return result.astype(jnp.bfloat16)


def solution(mesh):
    placed = (
        P(None, None, "freq", "pos"),
        P("freq", "pos", None),
        P("pos", "freq", None),
        P("pos", None),
    )
    return jax.shard_map(
        on_device, mesh=mesh, in_specs=placed, out_specs=P("pos", "freq", None), check_vma=False
    )
```

profile of v0, /device:TPU:1, one launch (start us, length us, event | category | flops | bytes accessed | tf_op | source)
XLA Modules:
  0.0 542.1 jit_solution(4617371937418704932)
XLA Ops:
  6.5 0.0 all-reduce.3.cloned.1.call-start
  6.5 51.6 %all_to_all.36 = bf16[16,2,64,1024]{3,2,1,0:T(8,128)(2,1)S(1)} all-to-all(bf16[16,2,64,1024]{3,2,1,0:T(8,128)(2,1)} %param.4), channel_id=1, replica_groups=mesh['freq'=4,'pos'=8] {'freq'}, dimensions={0} | all-to-all | bytes 8388608 | tf_op jit(solution)/shard_map/all_to_all | solution.py:19
  58.1 2.5 copy.8
  60.5 18.1 %fusion.24 = f32[256,4,2,2048]{0,3,2,1:T(8,128)} fusion(bf16[4,2,256,1024]{3,2,1,0:T(8,128)(2,1)} %bitcast.55, bf16[4,1024,2048]{2,1,0:T(8,128)(2,1)} %param.5), kind=kOutput, calls=%fused_computation.36 | convolution fusion | flops 8589934592 | bytes 37748736 | tf_op jit(solution)/shard_map/fisk,fkr->sfir/dot_general | solution.py:23
  78.6 9.2 %slice_subtract_fusion = (f32[256,4,1,1024]{0,3,2,1:T(8,128)S(1)}, f32[256,4,1,1024]{0,3,2,1:T(8,128)}) fusion(f32[256,4,2,2048]{0,3,2,1:T(8,128)} %fusion.24), kind=kLoop, calls=%fused_computation.38 | loop fusion | flops 2097152 | bytes 25165824 | tf_op jit(solution)/shard_map/sub | solution.py:24
  87.8 6.3 %pad_maximum_fusion = f32[256,4,2,1024]{0,3,2,1:T(8,128)} fusion(f32[256,4,1,1024]{0,3,2,1:T(8,128)} %get-tuple-element.6, f32[256,4,1,1024]{0,3,2,1:T(8,128)S(1)} %get-tuple-element.5), kind=kLoop, calls=%fused_computation.35 | loop fusion | flops 2097152 | bytes 16777216 | tf_op jit(solution)/shard_map/stack | solution.py:26
  94.1 0.0 copy-start
  94.1 0.0 all-reduce.3.cloned.1.call-update
  94.1 272.0 %all-reduce.3.cloned.1.call-done = f32[256,4,2,1024]{0,3,2,1:T(8,128)} async-done(((f32[256,4,2,1024]{0,3,2,1:T(8,128)}), f32[256,4,2,1024]{0,3,2,1:T(8,128)}) %all-reduce.3.cloned.1.call-update) | async-done | bytes 8388624 | tf_op jit(solution)/shard_map/psum | solution.py:26
  366.1 3.3 constant_dynamic-slice_fusion
  369.5 5.3 copy.17
  374.7 6.5 %reshape.114 = f32[4,1,65536]{2,1,0:T(1,128)} reshape(f32[1024,4,2,32]{3,2,1,0:T(2,128)} %bitcast.52) | data formatting | bytes 2097152
  381.2 4.2 all-to-all-start.1
  385.4 0.0 copy-done
  385.4 0.2 fusion.38
  385.7 13.4 %all-to-all-done.1 = f32[4,1,65536]{2,1,0:T(1,128)S(1)} async-done(((f32[4,1,65536]{2,1,0:T(1,128)}), f32[4,1,65536]{2,1,0:T(1,128)S(1)}, u32[]{:S(2)}, u32[]{:S(2)}) %all-to-all-start.1) | async-done | bytes 1048608 | tf_op jit(solution)/shard_map/all_to_all | solution.py:30
  399.0 0.5 broadcast.120
  399.5 3.7 reduce
  403.2 5.7 %reshape.115 = f32[1024,4,2,32]{3,2,1,0:T(2,128)} reshape(f32[4,65536]{1,0:T(4,128)S(1)} %reduce) | data formatting | bytes 2097152
  408.9 5.3 copy.11
  414.2 0.4 all_to_all.33
  414.6 16.0 %convolution_bitcast_fusion = f32[32,256,512]{2,1,0:T(8,128)} fusion(f32[32,16,2,256]{3,1,2,0:T(8,128)S(1)} %all_to_all.33, f32[16,1,512]{2,0,1:T(8,128)S(1)} %get-tuple-element.19, f32[16,1,512]{2,0,1:T(8,128)S(1)} %get-tuple-element.18), kind=kOutput, calls=%fused_computation.34 | convolution fusion | flops 1610645504 | bytes 17891328 | tf_op jit(solution)/shard_map/sfir,fit->srt/dot_general | solution.py:32
  430.6 104.7 %fusion.23 = bf16[32,256,512]{2,1,0:T(8,128)(2,1)} fusion(f32[32,256,512]{2,1,0:T(8,128)} %convolution_bitcast_fusion, bf16[32,256,512]{2,1,0:T(8,128)(2,1)} %param.6, f32[32]{0:T(128)S(1)} %get-tuple-element.16, f32[32]{0:T(128)S(1)} %get-tuple-element.17, f32[32]{0:T(128)S(1)} %get-tuple-element.8, f32[32]{0:T(128)S(1)} %get-tuple-element.9, ...), kind=kLoop, calls=%fused_computation.33 | loop fusion | flops 100663296 | bytes 33555840 | tf_op jit(solution)/shard_map/convert_element_type | solution.py:39
  (2 shorter events, 0.0 us)
Async XLA Ops:
  6.5 359.6 %all-reduce.3.cloned.1.call-start = ((), (), s32[]{:S(2)}) async-start(), calls=%async_computation.2 | async-start | bytes 16777216 | tf_op jit(solution)/shard_map/psum | solution.py:26
  94.1 291.3 %copy-start = (f32[32,11]{0,1:T(8,128)S(1)}, f32[32,11]{0,1:T(8,128)}, u32[]{:S(2)}) copy-start(f32[32,11]{0,1:T(8,128)} %param.7) | copy-start | bytes 4228
  381.2 17.8 %all-to-all-start.1 = ((f32[4,1,65536]{2,1,0:T(1,128)}), f32[4,1,65536]{2,1,0:T(1,128)S(1)}, u32[]{:S(2)}, u32[]{:S(2)}) async-start(f32[4,1,65536]{2,1,0:T(1,128)} %reshape.114), calls=%async_computation.1 | async-start | bytes 2097152 | tf_op jit(solution)/shard_map/all_to_all | solution.py:30
Sparse Core Ops, SparseCore 0:
  94.2 271.8 all-reduce.2
where the time goes:
time: 543 us; the launch traced here: 542 us
  waiting for transfers between devices  285 us (52%)
  other arithmetic  124 us (23%)
  blocking collectives  51.6 us (10%)
  matrix products  34 us (6%)
  local copies, waits for them, and re-layouts  29.4 us (5%)
  between operations  13.4 us (2%)
    psum x1, waiting for transfers between devices, on_device(): summed = lax.psum(jnp.stack([real_part, imag_part], 2), 'pos')  272 us
    convert_element_type x1, other arithmetic, on_device(): return result.astype(jnp.bfloat16)  105 us
    all_to_all x1, blocking collectives, on_device(): lax.all_to_all(spectra, 'freq', split_axis=0, concat_axis=2, tiled=True)  51.6 us
    dot_general x1, matrix products, on_device(): jnp.einsum('fisk,fkr->sfir', regrouped, green, preferred_element_type=jnp...  18.1 us
    dot_general x1, matrix products, on_device(): jnp.einsum('sfir,fit->srt', spread, table, precision=lax.Precision.HIGHEST)  16 us
    all_to_all x1, waiting for transfers between devices, on_device(): lax.all_to_all(own_share, 'freq', split_axis=3, concat_axis=1, tiled=True)  13.4 us
    unnamed x4, local copies, waits for them, and re-layouts  12.2 us
  transfers between devices with their start and end apart: 2, of which 2 were waited for; matrix products, arithmetic and copies ran while one was open for 0% of the time, Pallas kernels for 0%

commit v1 on v0

v1 whole, which is shorter than its diff:
```python
import functools

import jax
import jax.numpy as jnp
from jax import lax
from jax.experimental import pallas as pl
from jax.experimental.pallas import tpu as pltpu
from jax.sharding import PartitionSpec as P

BAND_START = 32
MESH = pl.DeviceIdType.MESH
TINY = 2.0**-126
Y_LAG = 2
Z_LAG = 4
AHEAD = 2


def phase_table(first_freq, freq_count, total_freqs, samples):
    bins = BAND_START + first_freq + jnp.arange(freq_count, dtype=jnp.int32)
    sample_index = jnp.arange(samples, dtype=jnp.int32)
    phase = bins[:, None] * sample_index[None, :] % samples
    angle = 2.0 * jnp.pi / samples * phase.astype(jnp.float32)
    scale = 1.0 / jnp.sqrt(jnp.float32(total_freqs))
    return jnp.stack([jnp.cos(angle), -jnp.sin(angle)], 1) * scale


def encode(x):
    x2 = (x * x) * 16.0
    x4 = x2 * x2
    y = x4 * x4
    return jnp.where(x < 0, -y, y).astype(jnp.bfloat16)


def decode(code):
    y = code.astype(jnp.float32)
    half = lax.rsqrt(jnp.maximum(jnp.abs(y), TINY))
    quarter = lax.rsqrt(half)
    size = lax.rsqrt(quarter) * quarter * 0.25
    return jnp.where(y < 0, -size, size)


def gather_kernel(
    nq, npos, spectra, green, out, xs, gbuf, acc, keep, ysend, yrecv, zsend, zrecv, fin, finrecv,
    xss, xrs, xls, gs, yss, yrs, zss, zrs, fss, frs,
):
    floc = green.shape[0]
    shots = spectra.shape[2]
    depth = spectra.shape[3]
    half_cols = green.shape[2] // 2
    width = half_cols // nq
    own = shots * nq // npos
    line = npos // 2
    chunks = floc * nq
    q = lax.axis_index("freq")
    p = lax.axis_index("pos")
    y = lax.rem(p, 2)
    z = p // 2
    other = p + 1 - 2 * y

    def turn(start, step, size):
        return lax.rem(start + step, size)

    barrier = pltpu.get_barrier_semaphore()
    for d in range(1, nq):
        pl.semaphore_signal(barrier, inc=1, device_id={"freq": turn(q, d, nq)}, device_id_type=MESH)
    pl.semaphore_signal(barrier, inc=1, device_id={"pos": other}, device_id_type=MESH)
    for d in range(1, line):
        pl.semaphore_signal(
            barrier, inc=1, device_id={"pos": turn(z, d, line) * 2 + y}, device_id_type=MESH
        )
    pl.semaphore_wait(barrier, nq - 1 + 1 + line - 1)

    def green_copy(f):
        return pltpu.make_async_copy(green.at[f], gbuf.at[lax.rem(f, 2)], gs.at[lax.rem(f, 2)])

    def own_spectra(f):
        return pltpu.make_async_copy(spectra.at[q * floc + f], xs.at[f, q], xls.at[f])

    def send_spectra(f, target):
        return pltpu.make_async_remote_copy(
            src_ref=spectra.at[target * floc + f],
            dst_ref=xs.at[f, q],
            send_sem=xss.at[f, target],
            recv_sem=xrs.at[f, q],
            device_id={"freq": target},
            device_id_type=MESH,
        )

    def recv_spectra(f, source):
        return pltpu.make_async_remote_copy(
            src_ref=spectra.at[q * floc + f],
            dst_ref=xs.at[f, source],
            send_sem=xss.at[f, source],
            recv_sem=xrs.at[f, source],
            device_id={"freq": source},
            device_id_type=MESH,
        )

    def start_spectra(f):
        for d in (2, 1, 3) if nq == 4 else range(1, nq):
            send_spectra(f, turn(q, d, nq)).start()

    def y_copy(n):
        return pltpu.make_async_remote_copy(
            src_ref=ysend.at[n],
            dst_ref=yrecv.at[n],
            send_sem=yss.at[n],
            recv_sem=yrs.at[n],
            device_id={"pos": other},
            device_id_type=MESH,
        )

    def z_copy(n, there, slot):
        return pltpu.make_async_remote_copy(
            src_ref=zsend.at[n, there],
            dst_ref=zrecv.at[n, slot],
            send_sem=zss.at[n, there],
            recv_sem=zrs.at[n, slot],
            device_id={"pos": there * 2 + y},
            device_id_type=MESH,
        )

    def fin_copy(f, there, slot):
        return pltpu.make_async_remote_copy(
            src_ref=fin.at[f, there],
            dst_ref=finrecv.at[slot, f],
            send_sem=fss.at[f, there],
            recv_sem=frs.at[slot, f],
            device_id={"freq": there},
            device_id_type=MESH,
        )

    for f in range(min(AHEAD, floc)):
        start_spectra(f)
    for f in range(floc):
        own_spectra(f).start()
    for f in range(min(2, floc)):
        green_copy(f).start()

    def multiply(n):
        f = n // nq
        d = lax.rem(n, nq)
        col = turn(q, d + 1, nq)

        @pl.when(d == 0)
        def _():
            own_spectra(f).wait()
            for step in range(1, nq):
                recv_spectra(f, turn(q, step, nq)).wait_recv()

            @pl.when(f + AHEAD < floc)
            def _():
                start_spectra(f + AHEAD)

            green_copy(f).wait()

            @pl.when((f >= 1) & (f + 1 < floc))
            def _():
                green_copy(f + 1).start()

        left = xs[f].reshape(nq * 2 * shots, depth)
        slot = lax.rem(f, 2)
        for part in range(2):
            columns = pl.ds(pl.multiple_of(part * half_cols + col * width, 128), width)
            acc[part] = jnp.dot(left, gbuf[slot, :, columns], preferred_element_type=jnp.float32)

        for there in range(line):
            for mine in (True, False):
                shot = (there * 2 + (y if mine else 1 - y)) * own
                row = (shot // shots) * (2 * shots) + lax.rem(shot, shots)
                re_rows = pl.ds(pl.multiple_of(row, 16), own)
                im_rows = pl.ds(pl.multiple_of(row + shots, 16), own)
                real = acc[0, re_rows] - acc[1, im_rows]
                imag = acc[1, re_rows] + acc[0, im_rows]
                if mine:
                    keep[n, there, 0] = real
                    keep[n, there, 1] = imag
                else:
                    ysend[n, there, 0] = encode(real)
                    ysend[n, there, 1] = encode(imag)
        y_copy(n).start()

    def pair(n):
        y_copy(n).wait_recv()
        for d in range(1, line):
            there = turn(z, d, line)
            zsend[n, there] = encode(keep[n, there] + decode(yrecv[n, there]))
            z_copy(n, there, z).start()
        keep[n, z] = keep[n, z] + decode(yrecv[n, z])

    def finish(n):
        f = n // nq
        d = lax.rem(n, nq)
        col = turn(q, d + 1, nq)
        total = keep[n, z]
        for step in range(1, line):
            source = turn(z, step, line)
            z_copy(n, source, source).wait_recv()
            total = total + decode(zrecv[n, source])

        @pl.when(d == nq - 1)
        def _():
            finrecv[q, f] = total

        @pl.when(d < nq - 1)
        def _():
            fin[f, col] = total
            fin_copy(f, col, q).start()

    def step(n, carry):
        @pl.when(n < chunks)
        def _():
            multiply(n)

        @pl.when((n >= Y_LAG) & (n < chunks + Y_LAG))
        def _():
            pair(n - Y_LAG)

        @pl.when(n >= Z_LAG)
        def _():
            finish(n - Z_LAG)

        return carry

    lax.fori_loop(0, chunks + Z_LAG, step, 0)

    def wait_sends(n, carry):
        y_copy(n).wait_send()
        for d in range(1, line):
            z_copy(n, turn(z, d, line), z).wait_send()
        return carry

    lax.fori_loop(0, chunks, wait_sends, 0)

    def wait_freq(f, carry):
        for d in range(1, nq):
            peer = turn(q, d, nq)
            send_spectra(f, peer).wait_send()
            fin_copy(f, peer, q).wait_send()
            fin_copy(f, peer, peer).wait_recv()
        return carry

    lax.fori_loop(0, floc, wait_freq, 0)
    out[...] = finrecv[...]


def gathered(spectra, green, nq, npos):
    total, _, shots, depth = spectra.shape
    floc = green.shape[0]
    half_cols = green.shape[2] // 2
    width = half_cols // nq
    own = shots * nq // npos
    line = npos // 2
    chunks = floc * nq
    f32, bf16 = jnp.float32, jnp.bfloat16
    dma = pltpu.SemaphoreType.DMA
    return pl.pallas_call(
        functools.partial(gather_kernel, nq, npos),
        out_shape=jax.ShapeDtypeStruct((nq, floc, 2, own, width), f32),
        in_specs=[pl.BlockSpec(memory_space=pl.ANY)] * 2,
        out_specs=pl.BlockSpec(memory_space=pltpu.VMEM),
        scratch_shapes=[
            pltpu.VMEM((floc, nq, 2, shots, depth), bf16),
            pltpu.VMEM((2, depth, 2 * half_cols), bf16),
            pltpu.VMEM((2, nq * 2 * shots, width), f32),
            pltpu.VMEM((chunks, line, 2, own, width), f32),
            pltpu.VMEM((chunks, line, 2, own, width), bf16),
            pltpu.VMEM((chunks, line, 2, own, width), bf16),
            pltpu.VMEM((chunks, line, 2, own, width), bf16),
            pltpu.VMEM((chunks, line, 2, own, width), bf16),
            pltpu.VMEM((floc, nq, 2, own, width), f32),
            pltpu.VMEM((nq, floc, 2, own, width), f32),
            dma((floc, nq)),
            dma((floc, nq)),
            dma((floc,)),
            dma((2,)),
            dma((chunks,)),
            dma((chunks,)),
            dma((chunks, line)),
            dma((chunks, line)),
            dma((floc, nq)),
            dma((nq, floc)),
        ],
        compiler_params=pltpu.CompilerParams(
            collective_id=0, has_side_effects=True, vmem_limit_bytes=56 * 2**20
        ),
        name="gather_sum",
    )(spectra, green)


def subtract_kernel(pred, table, recorded, out):
    swapped = jnp.swapaxes(pred[...], 0, 1)
    for s in range(out.shape[0]):
        value = swapped[s]
        top = value.astype(jnp.bfloat16)
        low = (value - top.astype(jnp.float32)).astype(jnp.bfloat16)
        wave = table[s]
        wave_top = wave.astype(jnp.bfloat16)
        wave_low = (wave - wave_top.astype(jnp.float32)).astype(jnp.bfloat16)
        left = jnp.concatenate([top, top, low], 0)
        right = jnp.concatenate([wave_top, wave_low, wave_top], 0)
        filtered = lax.dot_general(
            left, right, (((0,), (0,)), ((), ())), preferred_element_type=jnp.float32
        )
        out[s] = (recorded[s].astype(jnp.float32) - filtered).astype(jnp.bfloat16)


def subtract(pred, table, recorded):
    rows, own, width = pred.shape
    samples = recorded.shape[2]
    group = 8
    return pl.pallas_call(
        subtract_kernel,
        out_shape=jax.ShapeDtypeStruct(recorded.shape, jnp.bfloat16),
        grid=(own // group,),
        in_specs=[
            pl.BlockSpec((rows, group, width), lambda i: (0, i, 0)),
            pl.BlockSpec((group, rows, samples), lambda i: (i, 0, 0)),
            pl.BlockSpec((group, width, samples), lambda i: (i, 0, 0)),
        ],
        out_specs=pl.BlockSpec((group, width, samples), lambda i: (i, 0, 0)),
        compiler_params=pltpu.CompilerParams(vmem_limit_bytes=48 * 2**20),
        name="subtract",
    )(pred, table, recorded)


def on_device(nq, npos, spectra, green, recorded, filter_taps):
    samples = recorded.shape[2]
    total_freqs = spectra.shape[0]
    tap_count = filter_taps.shape[1]
    margin = (tap_count - 1) // 2
    table = phase_table(0, total_freqs, total_freqs, samples).reshape(2 * total_freqs, samples)
    padded = jnp.pad(table, ((0, 0), (margin, margin)))
    shifted = jnp.stack([padded[:, lag : lag + samples] for lag in range(tap_count)])
    waves = jnp.einsum("sl,lft->sft", filter_taps, shifted, precision=lax.Precision.HIGHEST)
    share = gathered(spectra, green, nq, npos)
    pred = share.reshape(2 * total_freqs, share.shape[3], share.shape[4])
    return subtract(pred, waves, recorded)


def solution(mesh):
    placed = (
        P(None, None, "freq", "pos"),
        P("freq", "pos", None),
        P("pos", "freq", None),
        P("pos", None),
    )
    return jax.shard_map(
        functools.partial(on_device, mesh.shape["freq"], mesh.shape["pos"]),
        mesh=mesh,
        in_specs=placed,
        out_specs=P("pos", "freq", None),
        check_vma=False,
    )
```

time: 543 us -> 89.7 us (0.17)
  waiting for transfers between devices: 285 us -> 0 us
  other arithmetic: 124 us -> 0.23 us
  Pallas kernels: 0 us -> 82.5 us
  blocking collectives: 51.6 us -> 0 us
  matrix products: 34 us -> 1.94 us
  local copies, waits for them, and re-layouts: 29.4 us -> 4.73 us
  between operations: 13.4 us -> 0.16 us
    psum x1 -> x0, waiting for transfers between devices: 272 us -> none  [on_device(): summed = lax.psum(jnp.stack([real_part, imag_part], 2), 'pos')]
    convert_element_type x1 -> x0, other arithmetic: 105 us -> none  [on_device(): return result.astype(jnp.bfloat16)]
    pallas_call x0 -> x2, Pallas kernels: none -> 82.5 us  [the longest x1 74.2 us: gathered(): pl.pallas_call(functools.partial(gather_kernel, nq, npos), out_shape=jax....]
    all_to_all x1 -> x0, blocking collectives: 51.6 us -> none  [on_device(): lax.all_to_all(spectra, 'freq', split_axis=0, concat_axis=2, tiled=True)]
    dot_general x2 -> x1, matrix products: 34 us -> 1.94 us  [on_device(): jnp.einsum('sl,lft->sft', filter_taps, shifted, precision=lax.Precision.H...]
    all_to_all x1 -> x0, waiting for transfers between devices: 13.4 us -> none  [on_device(): lax.all_to_all(own_share, 'freq', split_axis=3, concat_axis=1, tiled=True)]
    unnamed x4, local copies, waits for them, and re-layouts: 12.2 us -> 1.22 us
    sub x1 -> x0, other arithmetic: 9.17 us -> none  [on_device(): real_part = product[:, :, 0, :half_cols] - product[:, :, 1, half_cols:]]
  transfers between devices with their start and end apart: 2 -> 0, of which waited for: 2 -> 0; matrix products, arithmetic and copies ran while one was open for 0% -> 0% of each run, Pallas kernels for 0% -> 0%
where the time goes in v1:
time: 89.7 us; the launch traced here: 89.6 us
  Pallas kernels  82.5 us (92%)
  local copies, waits for them, and re-layouts  4.73 us (5%)
  matrix products  1.94 us (2%)
    pallas_call x1, Pallas kernels, gathered(): pl.pallas_call(functools.partial(gather_kernel, nq, npos), out_shape=jax....  74.2 us
    pallas_call x1, Pallas kernels, subtract(): pl.pallas_call(subtract_kernel, out_shape=jax.ShapeDtypeStruct(recorded.s...  8.32 us
    dot_general x1, matrix products, on_device(): jnp.einsum('sl,lft->sft', filter_taps, shifted, precision=lax.Precision.H...  1.94 us
    another operation x11, local copies, waits for them, and re-layouts, on_device(): jnp.stack([padded[:, lag:lag + samples] for lag in range(tap_count)])  1.85 us

profile of v1, /device:TPU:1, one launch (start us, length us, event | category | flops | bytes accessed | tf_op | source)
XLA Modules:
  0.0 89.6 jit_solution(7839485100441041171)
XLA Ops:
  0.0 0.0 copy-start
  0.0 0.2 fusion.15
  0.2 0.1 copy.25
  0.3 0.1 mul.78
  0.5 0.2 pad_slice_fusion
  0.8 0.1 copy.28
  0.8 0.1 copy.29
  0.9 0.1 copy.30
  1.0 0.1 copy.31
  1.1 0.1 copy.33
  1.1 0.1 copy.34
  1.2 0.1 copy.35
  1.3 0.1 copy.36
  1.4 0.1 copy.27
  1.5 1.2 %stack.50 = f32[11,32,512]{2,0,1:T(8,128)S(1)} concatenate(f32[1,32,512]{2,0,1:T(1,128)S(1)} %copy.27, f32[1,32,512]{2,0,1:T(1,128)S(1)} %copy.28, f32[1,32,512]{2,0,1:T(1,128)S(1)} %copy.29, f32[1,32,512]{2,0,1:T(1,128)S(1)} %copy.30, f32[1,32,512]{2,0,1:T(1,128)S(1)} %copy.31, f32[1,32,512]{2,0,1:T(1,128)S(1)} %mul.78, f32[1,32,512]{2,0,1:T(1,128)S(1)} %copy.33, ...), dimensions={0} | concatenate | bytes 1441792 | tf_op jit(solution)/shard_map/stack | solution.py:334
  2.6 0.0 copy-done
  2.7 1.9 %fusion.16 = f32[32,512,32]{1,2,0:T(8,128)S(1)} fusion(f32[11,32,512]{2,0,1:T(8,128)S(1)} %stack.50, f32[32,11]{0,1:T(8,128)S(1)} %copy-done), kind=kOutput, calls=%fused_computation.32 | convolution fusion | flops 69206016 | bytes 2819456 | tf_op jit(solution)/shard_map/sl,lft->sft/dot_general | solution.py:335
  4.6 1.2 %copy.39 = f32[32,512,32]{1,0,2:T(8,128)S(1)} copy(f32[32,512,32]{1,2,0:T(8,128)S(1)} %fusion.16) | data formatting | bytes 4194304 | tf_op jit(solution)/shard_map/sl,lft->sft/dot_general | solution.py:335
  5.8 74.2 %gather_sum.1 = f32[4,4,2,32,256]{4,3,2,1,0:T(8,128)} custom-call(bf16[16,2,64,1024]{3,2,1,0:T(8,128)(2,1)} %spectra.1, bf16[4,1024,2048]{2,1,0:T(8,128)(2,1)} %green.1), custom_call_target="tpu_custom_call" | custom-call | tf_op jit(solution)/shard_map/gather_sum/pallas_call | solution.py:257
  80.0 0.0 copy-start.1
  80.0 1.2 %copy-done.1 = f32[4,4,2,32,256]{4,3,2,1,0:T(8,128)S(1)} copy-done((f32[4,4,2,32,256]{4,3,2,1,0:T(8,128)S(1)}, f32[4,4,2,32,256]{4,3,2,1,0:T(8,128)}, u32[]{:S(2)}) %copy-start.1) | copy-done | bytes 1048600
  81.2 8.3 %subtract.1 = bf16[32,256,512]{2,1,0:T(8,128)(2,1)} custom-call(f32[32,32,256]{2,1,0:T(8,128)S(1)} %bitcast.27, f32[32,32,512]{2,1,0:T(8,128)S(1)} %bitcast.26, bf16[32,256,512]{2,1,0:T(8,128)(2,1)} %recorded.1), custom_call_target="tpu_custom_call" | custom-call | tf_op jit(solution)/shard_map/subtract/pallas_call | solution.py:312
  (4 shorter events, 0.1 us)
Async XLA Ops:
  0.0 2.6 %copy-start = (f32[32,11]{0,1:T(8,128)S(1)}, f32[32,11]{0,1:T(8,128)}, u32[]{:S(2)}) copy-start(f32[32,11]{0,1:T(8,128)} %param.7) | copy-start | bytes 4228
  80.0 1.2 %copy-start.1 = (f32[4,4,2,32,256]{4,3,2,1,0:T(8,128)S(1)}, f32[4,4,2,32,256]{4,3,2,1,0:T(8,128)}, u32[]{:S(2)}) copy-start(f32[4,4,2,32,256]{4,3,2,1,0:T(8,128)} %gather_sum.1) | copy-start | bytes 3145732

commit v2 on v1

--- a/solution.py
+++ b/solution.py
@@ -2,6 +2,7 @@
 
 import jax
 import jax.numpy as jnp
+import numpy as np
 from jax import lax
 from jax.experimental import pallas as pl
 from jax.experimental.pallas import tpu as pltpu
@@ -16,12 +17,10 @@
 
 
 def phase_table(first_freq, freq_count, total_freqs, samples):
-    bins = BAND_START + first_freq + jnp.arange(freq_count, dtype=jnp.int32)
-    sample_index = jnp.arange(samples, dtype=jnp.int32)
-    phase = bins[:, None] * sample_index[None, :] % samples
-    angle = 2.0 * jnp.pi / samples * phase.astype(jnp.float32)
-    scale = 1.0 / jnp.sqrt(jnp.float32(total_freqs))
-    return jnp.stack([jnp.cos(angle), -jnp.sin(angle)], 1) * scale
+    bins = BAND_START + first_freq + np.arange(freq_count)
+    phase = bins[:, None] * np.arange(samples)[None, :] % samples
+    angle = 2.0 * np.pi / samples * phase
+    return (np.stack([np.cos(angle), -np.sin(angle)], 1) / np.sqrt(total_freqs)).astype(np.float32)
 
 
 def encode(x):
@@ -40,7 +39,7 @@
 
 
 def gather_kernel(
-    nq, npos, spectra, green, out, xs, gbuf, acc, keep, ysend, yrecv, zsend, zrecv, fin, finrecv,
+    nq, npos, spectra, green, taps, shifted, out, waves, xs, gbuf, acc, keep, ysend, yrecv, zsend, zrecv, fin, finrecv,
     xss, xrs, xls, gs, yss, yrs, zss, zrs, fss, frs,
 ):
     floc = green.shape[0]
@@ -137,6 +136,17 @@
     for f in range(min(2, floc)):
         green_copy(f).start()
 
+    def wave(s, carry):
+        total = taps[0, s] * shifted[0]
+        for lag in range(1, shifted.shape[0]):
+            total = total + taps[lag, s] * shifted[lag]
+        top = total.astype(jnp.bfloat16)
+        waves[s, 0] = top
+        waves[s, 1] = (total - top.astype(jnp.float32)).astype(jnp.bfloat16)
+        return carry
+
+    lax.fori_loop(0, own, wave, 0)
+
     def multiply(n):
         f = n // nq
         d = lax.rem(n, nq)
@@ -244,7 +254,7 @@
     out[...] = finrecv[...]
 
 
-def gathered(spectra, green, nq, npos):
+def gathered(spectra, green, taps, shifted, nq, npos):
     total, _, shots, depth = spectra.shape
     floc = green.shape[0]
     half_cols = green.shape[2] // 2
@@ -256,9 +266,17 @@
     dma = pltpu.SemaphoreType.DMA
     return pl.pallas_call(
         functools.partial(gather_kernel, nq, npos),
-        out_shape=jax.ShapeDtypeStruct((nq, floc, 2, own, width), f32),
-        in_specs=[pl.BlockSpec(memory_space=pl.ANY)] * 2,
-        out_specs=pl.BlockSpec(memory_space=pltpu.VMEM),
+        out_shape=(
+            jax.ShapeDtypeStruct((nq, floc, 2, own, width), f32),
+            jax.ShapeDtypeStruct((own, 2, *shifted.shape[1:]), bf16),
+        ),
+        in_specs=[
+            pl.BlockSpec(memory_space=pl.ANY),
+            pl.BlockSpec(memory_space=pl.ANY),
+            pl.BlockSpec(memory_space=pltpu.SMEM),
+            pl.BlockSpec(memory_space=pltpu.VMEM),
+        ],
+        out_specs=[pl.BlockSpec(memory_space=pltpu.VMEM)] * 2,
         scratch_shapes=[
             pltpu.VMEM((floc, nq, 2, shots, depth), bf16),
             pltpu.VMEM((2, depth, 2 * half_cols), bf16),
@@ -285,7 +303,7 @@
             collective_id=0, has_side_effects=True, vmem_limit_bytes=56 * 2**20
         ),
         name="gather_sum",
-    )(spectra, green)
+    )(spectra, green, taps, shifted)
 
 
 def subtract_kernel(pred, table, recorded, out):
@@ -294,9 +312,8 @@
         value = swapped[s]
         top = value.astype(jnp.bfloat16)
         low = (value - top.astype(jnp.float32)).astype(jnp.bfloat16)
-        wave = table[s]
-        wave_top = wave.astype(jnp.bfloat16)
-        wave_low = (wave - wave_top.astype(jnp.float32)).astype(jnp.bfloat16)
+        wave_top = table[s, 0]
+        wave_low = table[s, 1]
         left = jnp.concatenate([top, top, low], 0)
         right = jnp.concatenate([wave_top, wave_low, wave_top], 0)
         filtered = lax.dot_general(
@@ -315,11 +332,11 @@
         grid=(own // group,),
         in_specs=[
             pl.BlockSpec((rows, group, width), lambda i: (0, i, 0)),
-            pl.BlockSpec((group, rows, samples), lambda i: (i, 0, 0)),
+            pl.BlockSpec((group, 2, rows, samples), lambda i: (i, 0, 0, 0)),
             pl.BlockSpec((group, width, samples), lambda i: (i, 0, 0)),
         ],
         out_specs=pl.BlockSpec((group, width, samples), lambda i: (i, 0, 0)),
-        compiler_params=pltpu.CompilerParams(vmem_limit_bytes=48 * 2**20),
+        compiler_params=pltpu.CompilerParams(vmem_limit_bytes=62 * 2**20),
         name="subtract",
     )(pred, table, recorded)
 
@@ -330,10 +347,9 @@
     tap_count = filter_taps.shape[1]
     margin = (tap_count - 1) // 2
     table = phase_table(0, total_freqs, total_freqs, samples).reshape(2 * total_freqs, samples)
-    padded = jnp.pad(table, ((0, 0), (margin, margin)))
-    shifted = jnp.stack([padded[:, lag : lag + samples] for lag in range(tap_count)])
-    waves = jnp.einsum("sl,lft->sft", filter_taps, shifted, precision=lax.Precision.HIGHEST)
-    share = gathered(spectra, green, nq, npos)
+    padded = np.pad(table, ((0, 0), (margin, margin)))
+    shifted = np.stack([padded[:, lag : lag + samples] for lag in range(tap_count)])
+    share, waves = gathered(spectra, green, filter_taps.T, jnp.asarray(shifted), nq, npos)
     pred = share.reshape(2 * total_freqs, share.shape[3], share.shape[4])
     return subtract(pred, waves, recorded)
 

time: 89.7 us -> 85.1 us (0.949)
  local copies, waits for them, and re-layouts: 4.73 us -> 0 us
  Pallas kernels: 82.5 us -> 84.9 us
  matrix products: 1.94 us -> 0 us
    dot_general x1 -> x0, matrix products: 1.94 us -> none  [on_device(): jnp.einsum('sl,lft->sft', filter_taps, shifted, precision=lax.Precision.H...]
    another operation x11 -> x0, local copies, waits for them, and re-layouts: 1.85 us -> none  [on_device(): jnp.stack([padded[:, lag:lag + samples] for lag in range(tap_count)])]
    pallas_call x1, Pallas kernels: 74.2 us -> 75.9 us  [gathered(): pl.pallas_call(functools.partial(gather_kernel, nq, npos), out_shape=(jax...]
    unnamed x4 -> x0, local copies, waits for them, and re-layouts: 1.22 us -> none
    dot_general x1 -> x0, local copies, waits for them, and re-layouts: 1.22 us -> none  [on_device(): jnp.einsum('sl,lft->sft', filter_taps, shifted, precision=lax.Precision.H...]
where the time goes in v2:
time: 85.1 us; the launch traced here: 84.9 us
  Pallas kernels  84.9 us (100%)
    pallas_call x1, Pallas kernels, gathered(): pl.pallas_call(functools.partial(gather_kernel, nq, npos), out_shape=(jax...  75.9 us
    pallas_call x1, Pallas kernels, subtract(): pl.pallas_call(subtract_kernel, out_shape=jax.ShapeDtypeStruct(recorded.s...  8.95 us

profile of v2, /device:TPU:1, one launch (start us, length us, event | category | flops | bytes accessed | tf_op | source)
XLA Modules:
  0.0 84.9 jit_solution(16381501249057825810)
XLA Ops:
  0.0 75.9 %gather_sum.1 = (f32[4,4,2,32,256]{4,3,2,1,0:T(8,128)}, bf16[32,2,32,512]{3,2,1,0:T(8,128)(2,1)}) custom-call(bf16[16,2,64,1024]{3,2,1,0:T(8,128)(2,1)} %spectra.1, bf16[4,1024,2048]{2,1,0:T(8,128)(2,1)} %green.1, f32[11,32]{1,0:T(8,128)} %bitcast.3, f32[11,32,512]{2,1,0:T(8,128)} %constant.2.clone.shifted), custom_call_target="tpu_custom_call" | custom-call | tf_op jit(solution)/shard_map/gather_sum/pallas_call | solution.py:267
  75.9 9.0 %subtract.1 = bf16[32,256,512]{2,1,0:T(8,128)(2,1)} custom-call(f32[32,32,256]{2,1,0:T(8,128)} %bitcast.2, bf16[32,2,32,512]{3,2,1,0:T(8,128)(2,1)} %get-tuple-element.8.table, bf16[32,256,512]{2,1,0:T(8,128)(2,1)} %recorded.1), custom_call_target="tpu_custom_call" | custom-call | tf_op jit(solution)/shard_map/subtract/pallas_call | solution.py:329
